TPU v7x, 512 devices: a whole 4x4x16 slice. The times are simulated.
512 devices in a mesh: pairs: 512 (over z, x, y, core).
Axes of the slice: x: 4, y: 4, z: 16, core: 2. Of those that a mesh axis runs over, the one named last changes fastest.
Arguments:
- coeffs: bfloat16 [32768, 128, 128], P('pairs'), may hold values from -6 to 6
- target_box: int32 [3, 32768], P(None, 'pairs'), may hold values from 0 to 4095
- source_box: int32 [3, 32768], P(None, 'pairs'), may hold values from 0 to 4095
- interp: bfloat16 [3, 2, 2, 128, 128], replicated, may hold values from -0.375 to 0.375
Outputs:
- result: bfloat16 [32768, 128, 128], P('pairs')
All inputs are finite; a program needn't handle non-finite values.
Results may differ from a plain program's by a relative error of at most 0.02.
Values may be sent and summed in bfloat16 or wider, within the bound.
A program may use at most 64 MiB of HBM per device.

v0:
```python
import math

import jax
import jax.numpy as jnp
from jax import lax
from jax.sharding import PartitionSpec as P


def partner(x, axis, stride):
    return lax.ppermute(x, axis, [(i, i ^ 1 << stride) for i in range(lax.axis_size(axis))])


def rotate(current, target_box, source_box, rung_index):
    offsets = jnp.mod(target_box[rung_index] - source_box[rung_index], 4096).astype(jnp.float32)
    angles = offsets * (2.0 * math.pi / 4096.0)
    cosine = jnp.cos(angles)[:, None, None]
    sines = jnp.sin(angles)[:, None, None]
    widened = current.astype(jnp.float32)
    rank_count = widened.shape[-1] // 2
    real_part = widened[..., :rank_count]
    imag_part = widened[..., rank_count:]
    turned = jnp.concatenate(
        [cosine * real_part - sines * imag_part, sines * real_part + cosine * imag_part], axis=-1
    )
    return turned.astype(jnp.bfloat16)


def combine(kept, received, level_weights, side_bit):
    own_weights = lax.dynamic_index_in_dim(level_weights, side_bit, 1, keepdims=False)
    far_weights = lax.dynamic_index_in_dim(level_weights, 1 - side_bit, 1, keepdims=False)
    combined = jnp.einsum("knd,tde->ktne", kept, own_weights, preferred_element_type=jnp.float32)
    return combined + jnp.einsum(
        "knd,tde->ktne", received, far_weights, preferred_element_type=jnp.float32
    )


def body(coeffs, target_box, source_box, interp):
    slot_count, vectors, columns = coeffs.shape
    half_rows = slot_count // 2
    log_count = lax.axis_size("pairs").bit_length() - 1
    position = lax.axis_index("pairs")
    current = coeffs
    for rung_index in range(interp.shape[0]):
        bit_place = log_count - 1 - rung_index
        side_bit = jnp.right_shift(position, bit_place) & 1
        rotated = rotate(current, target_box, source_box, rung_index)
        kept = lax.dynamic_slice_in_dim(rotated, side_bit * half_rows, half_rows, 0)
        outgoing = lax.dynamic_slice_in_dim(rotated, (1 - side_bit) * half_rows, half_rows, 0)
        level_weights = interp[rung_index]
        received = partner(outgoing, "pairs", bit_place)
        combined = combine(kept, received, level_weights, side_bit)
        current = combined.reshape(slot_count, vectors, columns).astype(jnp.bfloat16)
    return current


def solution(mesh):
    placed = (P("pairs", None, None), P(None, "pairs"), P(None, "pairs"), P())
    return jax.shard_map(
        body, mesh=mesh, in_specs=placed, out_specs=P("pairs", None, None), check_vma=False
    )
```

profile of v0, /device:TPU:1, one launch (start us, length us, event | category | flops | bytes accessed | tf_op | source)
XLA Modules:
  0.0 285.1 jit_solution(8173714216062048057)
XLA Ops:
  0.0 0.9 fusion.49
  0.9 4.1 %convert_element_type.76 = f32[64,128,128]{2,1,0:T(8,128)} convert(bf16[64,128,128]{2,1,0:T(8,128)(2,1)} %param.4) | non-fusion elementwise | flops 1048576 | bytes 6291456 | tf_op jit(solution)/shard_map/convert_element_type | solution.py:18
  5.0 5.1 %add_convert_fusion.5 = (bf16[64,128,64]{2,1,0:T(8,128)(2,1)S(1)}, bf16[64,128,64]{2,1,0:T(8,128)(2,1)S(1)}) fusion(f32[64,128,128]{2,1,0:T(8,128)} %convert_element_type.76, f32[64]{0:T(128)S(1)} %sin.21, f32[64]{0:T(128)S(1)} %get-tuple-element.20), kind=kLoop, calls=%fused_computation.9 | loop fusion | flops 4194304 | bytes 6291968 | tf_op jit(solution)/shard_map/convert.9
  10.1 1.7 fusion.11
  11.8 16.3 %collective-permute-start = (bf16[32,128,128]{2,1,0:T(8,128)(2,1)}, bf16[32,128,128]{2,1,0:T(8,128)(2,1)S(1)}, u32[]{:S(2)}, u32[]{:S(2)}) collective-permute-start(bf16[32,128,128]{2,1,0:T(8,128)(2,1)} %fusion.11), channel_id=1, source_target_pairs={{0,256},{1,257},{2,258},{3,259},{4,260},{5,261},{6,262},{7,263},{8... | collective-permute-start | bytes 3145736 | tf_op jit(solution)/shard_map/ppermute | solution.py:10
  28.1 1.1 fusion.55
  29.2 2.1 fusion.14
  31.3 32.5 %collective-permute-done = bf16[32,128,128]{2,1,0:T(8,128)(2,1)S(1)} collective-permute-done((bf16[32,128,128]{2,1,0:T(8,128)(2,1)}, bf16[32,128,128]{2,1,0:T(8,128)(2,1)S(1)}, u32[]{:S(2)}, u32[]{:S(2)}) %collective-permute-start) | collective-permute-done | bytes 1048608 | tf_op jit(solution)/shard_map/ppermute | solution.py:10
  63.8 2.7 convert_bitcast_fusion.1
  66.5 5.6 %copy.15 = f32[32,2,128,128]{3,2,1,0:T(8,128)} copy(f32[32,2,128,128]{2,3,0,1:T(8,128)} %convert_bitcast_fusion.1) | data formatting | bytes 8388608 | tf_op jit(solution)/shard_map/convert_element_type | solution.py:18
  72.2 5.1 %add_convert_fusion.3 = (bf16[64,128,64]{2,1,0:T(8,128)(2,1)S(1)}, bf16[64,128,64]{2,1,0:T(8,128)(2,1)S(1)}) fusion(f32[64,128,128]{2,1,0:T(8,128)} %bitcast.85, f32[64]{0:T(128)S(1)} %sin.22, f32[64]{0:T(128)S(1)} %get-tuple-element.22), kind=kLoop, calls=%fused_computation.6 | loop fusion | flops 4194304 | bytes 6291968 | tf_op jit(solution)/shard_map/convert.7
  77.3 1.7 fusion.6
  78.9 47.6 %collective-permute-start.1 = (bf16[32,128,128]{2,1,0:T(8,128)(2,1)}, bf16[32,128,128]{2,1,0:T(8,128)(2,1)S(1)}, u32[]{:S(2)}, u32[]{:S(2)}) collective-permute-start(bf16[32,128,128]{2,1,0:T(8,128)(2,1)} %fusion.6), channel_id=1, source_target_pairs={{0,128},{1,129},{2,130},{3,131},{4,132},{5,133},{6,134},{7,135},{8... | collective-permute-start | bytes 3145736 | tf_op jit(solution)/shard_map/ppermute | solution.py:10
  126.6 2.1 fusion.9
  128.7 87.4 %collective-permute-done.1 = bf16[32,128,128]{2,1,0:T(8,128)(2,1)S(1)} collective-permute-done((bf16[32,128,128]{2,1,0:T(8,128)(2,1)}, bf16[32,128,128]{2,1,0:T(8,128)(2,1)S(1)}, u32[]{:S(2)}, u32[]{:S(2)}) %collective-permute-start.1) | collective-permute-done | bytes 1048608 | tf_op jit(solution)/shard_map/ppermute | solution.py:10
  216.2 2.7 convert_bitcast_fusion
  218.9 5.6 %copy.17 = f32[32,2,128,128]{3,2,1,0:T(8,128)} copy(f32[32,2,128,128]{2,3,0,1:T(8,128)} %convert_bitcast_fusion) | data formatting | bytes 8388608 | tf_op jit(solution)/shard_map/convert_element_type | solution.py:18
  224.5 5.1 %add_convert_fusion.1 = (bf16[64,128,64]{2,1,0:T(8,128)(2,1)S(1)}, bf16[64,128,64]{2,1,0:T(8,128)(2,1)S(1)}) fusion(f32[64,128,128]{2,1,0:T(8,128)} %bitcast.84, f32[64]{0:T(128)S(1)} %sin.23, f32[64]{0:T(128)S(1)} %get-tuple-element.5), kind=kLoop, calls=%fused_computation.3 | loop fusion | flops 4194304 | bytes 6291968 | tf_op jit(solution)/shard_map/convert.5
  230.2 0.7 copy-done.2
  230.9 1.9 collective-permute-start.2
  232.9 2.1 fusion.4
  235.0 45.4 %collective-permute-done.2 = bf16[32,128,128]{2,1,0:T(8,128)(2,1)} collective-permute-done((bf16[32,128,128]{2,1,0:T(8,128)(2,1)S(1)}, bf16[32,128,128]{2,1,0:T(8,128)(2,1)}, u32[]{:S(2)}, u32[]{:S(2)}) %collective-permute-start.2) | collective-permute-done | bytes 1048608 | tf_op jit(solution)/shard_map/ppermute | solution.py:10
  280.4 2.0 fusion
  282.4 2.7 copy.19
  (9 shorter events, 0.7 us)
Async XLA Ops:
  10.1 1.7 copy-start
  11.8 52.1 %collective-permute-start = (bf16[32,128,128]{2,1,0:T(8,128)(2,1)}, bf16[32,128,128]{2,1,0:T(8,128)(2,1)S(1)}, u32[]{:S(2)}, u32[]{:S(2)}) collective-permute-start(bf16[32,128,128]{2,1,0:T(8,128)(2,1)} %fusion.11), channel_id=1, source_target_pairs={{0,256},{1,257},{2,258},{3,259},{4,260},{5,261},{6,262},{7,263},{8... | collective-permute-start | bytes 3145736 | tf_op jit(solution)/shard_map/ppermute | solution.py:10
  77.3 1.7 copy-start.1
  78.9 137.2 %collective-permute-start.1 = (bf16[32,128,128]{2,1,0:T(8,128)(2,1)}, bf16[32,128,128]{2,1,0:T(8,128)(2,1)S(1)}, u32[]{:S(2)}, u32[]{:S(2)}) collective-permute-start(bf16[32,128,128]{2,1,0:T(8,128)(2,1)} %fusion.6), channel_id=1, source_target_pairs={{0,128},{1,129},{2,130},{3,131},{4,132},{5,133},{6,134},{7,135},{8... | collective-permute-start | bytes 3145736 | tf_op jit(solution)/shard_map/ppermute | solution.py:10
  229.6 1.3 copy-start.2
  230.9 49.5 %collective-permute-start.2 = (bf16[32,128,128]{2,1,0:T(8,128)(2,1)S(1)}, bf16[32,128,128]{2,1,0:T(8,128)(2,1)}, u32[]{:S(2)}, u32[]{:S(2)}) collective-permute-start(bf16[32,128,128]{2,1,0:T(8,128)(2,1)S(1)} %fusion.1), channel_id=1, source_target_pairs={{0,64},{1,65},{2,66},{3,67},{4,68},{5,69},{6,70},{7,71},{8,72},{9,... | collective-permute-start | bytes 3145736 | tf_op jit(solution)/shard_map/ppermute | solution.py:10
where the time goes:
time: 286 us; the launch traced here: 285 us
  waiting for transfers between devices  165 us (58%)
  starting transfers between devices  65.8 us (23%)
  other arithmetic  24.1 us (8%)
  local copies, waits for them, and re-layouts  15.9 us (6%)
  matrix products  13.8 us (5%)
    ppermute x3, waiting for transfers between devices, partner(): lax.ppermute(x, axis, [(i, i ^ 1 << stride) for i in range(lax.axis_size(...  165 us
    ppermute x3, starting transfers between devices, partner(): lax.ppermute(x, axis, [(i, i ^ 1 << stride) for i in range(lax.axis_size(...  65.8 us
    another operation x3, other arithmetic  15.3 us
    convert_element_type x2, local copies, waits for them, and re-layouts, rotate(): widened = current.astype(jnp.float32)  11.3 us
    dot_general x3, matrix products, combine(): jnp.einsum('knd,tde->ktne', received, far_weights, preferred_element_type...  7.38 us
    dot_general x3, matrix products, combine(): jnp.einsum('knd,tde->ktne', kept, own_weights, preferred_element_type=jnp...  6.38 us
  transfers between devices with their start and end apart: 3, of which 3 were waited for; matrix products, arithmetic and copies ran while one was open for 3% of the time, Pallas kernels for 0%

commit v1 on v0

v1 whole, which is shorter than its diff:
```python
import functools
import math

import jax
import jax.numpy as jnp
from jax import lax
from jax.experimental import pallas as pl
from jax.experimental.pallas import tpu as pltpu
from jax.sharding import PartitionSpec as P

MESH = pl.DeviceIdType.MESH
GROUP = 8
FAR = (4, 3, -3, 2, -2, 1, -1)


def kernel(n, coeffs, tbox, sbox, interp, out, got, tab, tabs, phase, wcat,
           send, recv, tsend, trecv, own):
    stride = n // GROUP
    me = lax.axis_index("pairs")
    e_me = me // stride
    rest = me % stride

    def peer(d):
        return ((e_me + d + GROUP) % GROUP) * stride + rest

    def slot_copy(d, g):
        to = (e_me + d + GROUP) % GROUP
        return pltpu.make_async_remote_copy(
            src_ref=coeffs.at[to * GROUP + g],
            dst_ref=got.at[d % GROUP, g],
            send_sem=send.at[d % GROUP, g],
            recv_sem=recv.at[d % GROUP, g],
            device_id=(peer(d),),
            device_id_type=MESH,
        )

    def table_copy(d):
        return pltpu.make_async_remote_copy(
            src_ref=tab,
            dst_ref=tabs.at[d % GROUP],
            send_sem=tsend.at[d % GROUP],
            recv_sem=trecv.at[d % GROUP],
            device_id=(peer(d),),
            device_id_type=MESH,
        )

    barrier = pltpu.get_barrier_semaphore()
    for d in FAR:
        pl.semaphore_signal(barrier, inc=1, device_id=(peer(d),), device_id_type=MESH)
    own_copy = pltpu.make_async_copy(
        coeffs.at[pl.ds(e_me * GROUP, GROUP)], got.at[0], own.at[0]
    )
    own_copy.start()
    turn = ((tbox[...] - sbox[...]) & 4095).astype(jnp.float32) * (2.0 * math.pi / 4096.0)
    tab[0:3, :] = jnp.concatenate([jnp.cos(turn), jnp.sin(turn)], axis=1)
    tab[3:8, :] = jnp.zeros((5, 128), jnp.float32)
    pl.semaphore_wait(barrier, len(FAR))

    for d in FAR:
        table_copy(d).start()

    def start_slots(g, carry):
        for d in FAR:
            slot_copy(d, g).start()
        return carry

    lax.fori_loop(0, GROUP, start_slots, 0)

    for l in range(3):
        for t in range(2):
            for c in range(2):
                wcat[l, c * 128:(c + 1) * 128, t * 128:(t + 1) * 128] = interp[l, t, c]

    tabs[0] = tab[...]
    for d in FAR:
        table_copy(d).wait_recv()
    to_scalar = pltpu.make_async_copy(tabs, phase, own.at[1])
    to_scalar.start()
    to_scalar.wait()
    own_copy.wait()

    sign = jnp.where(lax.broadcasted_iota(jnp.int32, (1, 128), 1) < 64, -1.0, 1.0)
    f0, f1, f2 = e_me // 4, e_me // 2 % 2, e_me % 2

    def turned(x, e, l, slot):
        at = (e_me - e + GROUP) % GROUP
        c = phase[at, l, slot]
        s = phase[at, l, 64 + slot]
        return (c * x + (s * sign) * pltpu.roll(x, 64, 1)).astype(jnp.bfloat16)

    def level(l, pieces):
        rows = jnp.concatenate([jnp.concatenate(p, axis=1) for p in pieces], axis=0)
        return jnp.dot(rows, wcat[l], preferred_element_type=jnp.float32)

    def work(g, carry):
        for d in FAR:
            slot_copy(d, g).wait_recv()
        y = level(0, [
            [turned(got[(e_me - e + GROUP) % GROUP, g].astype(jnp.float32), e, 0,
                    e_me * 8 + g)
             for e in (e1 * 2 + e2, 4 + e1 * 2 + e2)]
            for e1 in range(2) for e2 in range(2)
        ])
        y = level(1, [
            [turned(y[(e1 * 2 + e2) * 128:(e1 * 2 + e2 + 1) * 128, t0 * 128:(t0 + 1) * 128],
                    f0 * 4 + e1 * 2 + e2, 1, f1 * 32 + f2 * 16 + g * 2 + t0)
             for e1 in range(2)]
            for e2 in range(2) for t0 in range(2)
        ])
        y = level(2, [
            [turned(y[(e2 * 2 + t0) * 128:(e2 * 2 + t0 + 1) * 128, t1 * 128:(t1 + 1) * 128],
                    f0 * 4 + f1 * 2 + e2, 2, f2 * 32 + g * 4 + t0 * 2 + t1)
             for e2 in range(2)]
            for t0 in range(2) for t1 in range(2)
        ])
        for t01 in range(4):
            for t2 in range(2):
                out[g * 8 + t01 * 2 + t2] = y[
                    t01 * 128:(t01 + 1) * 128, t2 * 128:(t2 + 1) * 128
                ].astype(jnp.bfloat16)
        return carry

    lax.fori_loop(0, GROUP, work, 0)

    def finish(g, carry):
        for d in FAR:
            slot_copy(d, g).wait_send()
        return carry

    for d in FAR:
        table_copy(d).wait_send()
    lax.fori_loop(0, GROUP, finish, 0)


def solution(mesh):
    n = mesh.shape["pairs"]

    def body(coeffs, target_box, source_box, interp):
        _, rows, columns = coeffs.shape
        dma = pltpu.SemaphoreType.DMA
        return pl.pallas_call(
            functools.partial(kernel, n),
            out_shape=jax.ShapeDtypeStruct(coeffs.shape, jnp.bfloat16),
            in_specs=[pl.BlockSpec(memory_space=pltpu.HBM)]
            + [pl.BlockSpec(memory_space=pltpu.VMEM)] * 3,
            out_specs=pl.BlockSpec(memory_space=pltpu.VMEM),
            scratch_shapes=[
                pltpu.VMEM((GROUP, GROUP, rows, columns), jnp.bfloat16),
                pltpu.VMEM((8, 128), jnp.float32),
                pltpu.VMEM((GROUP, 8, 128), jnp.float32),
                pltpu.SMEM((GROUP, 8, 128), jnp.float32),
                pltpu.VMEM((3, 256, 256), jnp.bfloat16),
                dma((GROUP, GROUP)),
                dma((GROUP, GROUP)),
                dma((GROUP,)),
                dma((GROUP,)),
                dma((2,)),
            ],
            compiler_params=pltpu.CompilerParams(
                collective_id=0, has_side_effects=True, vmem_limit_bytes=32 << 20
            ),
            name="butterfly",
        )(coeffs, target_box, source_box, interp)

    placed = (P("pairs", None, None), P(None, "pairs"), P(None, "pairs"), P())
    return jax.shard_map(
        body, mesh=mesh, in_specs=placed, out_specs=P("pairs", None, None), check_vma=False
    )
```

time: 286 us -> 116 us (0.41)
  waiting for transfers between devices: 165 us -> 0 us
  Pallas kernels: 0 us -> 110 us
  starting transfers between devices: 65.8 us -> 0 us
  other arithmetic: 24.1 us -> 0 us
  matrix products: 13.8 us -> 0 us
  local copies, waits for them, and re-layouts: 15.9 us -> 5.27 us
    ppermute x3 -> x0, waiting for transfers between devices: 165 us -> none  [partner(): lax.ppermute(x, axis, [(i, i ^ 1 << stride) for i in range(lax.axis_size(...]
    pallas_call x0 -> x1, Pallas kernels: none -> 110 us  [body(): pl.pallas_call(functools.partial(kernel, n), out_shape=jax.ShapeDtypeStru...]
    ppermute x3 -> x0, starting transfers between devices: 65.8 us -> none  [partner(): lax.ppermute(x, axis, [(i, i ^ 1 << stride) for i in range(lax.axis_size(...]
    another operation x3 -> x0, other arithmetic: 15.3 us -> none
    convert_element_type x3 -> x0, local copies, waits for them, and re-layouts: 14 us -> none  [the longest x2 11.3 us: rotate(): widened = current.astype(jnp.float32)]
    dot_general x6 -> x0, matrix products: 13.8 us -> none  [the longest x3 7.38 us: combine(): jnp.einsum('knd,tde->ktne', received, far_weights, preferred_element_type...]
    unnamed x6 -> x9, local copies, waits for them, and re-layouts: 0.73 us -> 5.27 us
    convert_element_type x1 -> x0, other arithmetic: 4.07 us -> none  [rotate(): widened = current.astype(jnp.float32)]
  transfers between devices with their start and end apart: 3 -> 0, of which waited for: 3 -> 0; matrix products, arithmetic and copies ran while one was open for 3% -> 0% of each run, Pallas kernels for 0% -> 0%
where the time goes in v1:
time: 116 us; the launch traced here: 115 us
  Pallas kernels  110 us (95%)
  local copies, waits for them, and re-layouts  5.27 us (5%)
    pallas_call x1, Pallas kernels, body(): pl.pallas_call(functools.partial(kernel, n), out_shape=jax.ShapeDtypeStru...  110 us
    unnamed x9, local copies, waits for them, and re-layouts  5.27 us

profile of v1, /device:TPU:1, one launch (start us, length us, event | category | flops | bytes accessed | tf_op | source)
XLA Modules:
  0.0 115.4 jit_solution(14517532546562222930)
XLA Ops:
  0.0 0.0 copy-start
  0.0 1.6 %copy-done = bf16[64,128,128]{2,1,0:T(8,128)(2,1)S(1)} copy-done((bf16[64,128,128]{2,1,0:T(8,128)(2,1)S(1)}, bf16[64,128,128]{2,1,0:T(8,128)(2,1)}, u32[]{:S(2)}) %copy-start) | copy-done | bytes 2097176
  1.6 0.0 copy-start.1
  1.6 1.0 copy-done.1
  2.6 0.0 copy-start.2
  2.6 0.7 copy-done.2
  3.3 0.0 copy-start.3
  3.3 0.7 copy-done.3
  4.0 110.1 %butterfly.1 = bf16[64,128,128]{2,1,0:T(8,128)(2,1)S(1)} custom-call(bf16[64,128,128]{2,1,0:T(8,128)(2,1)S(1)} %copy-done, s32[3,64]{1,0:T(4,128)S(1)} %copy-done.2, s32[3,64]{1,0:T(4,128)S(1)} %copy-done.3, bf16[3,2,2,128,128]{4,3,2,1,0:T(8,128)(2,1)S(1)} %copy-done.1), custom_call_target="tpu_custom_call" | custom-call | tf_op jit(solution)/shard_map/butterfly/pallas_call | solution.py:141
  114.1 1.3 %copy.6 = bf16[64,128,128]{2,1,0:T(8,128)(2,1)} copy(bf16[64,128,128]{2,1,0:T(8,128)(2,1)S(1)} %butterfly.1) | data formatting | bytes 4194304
Async XLA Ops:
  0.0 1.6 %copy-start = (bf16[64,128,128]{2,1,0:T(8,128)(2,1)S(1)}, bf16[64,128,128]{2,1,0:T(8,128)(2,1)}, u32[]{:S(2)}) copy-start(bf16[64,128,128]{2,1,0:T(8,128)(2,1)} %coeffs.1) | copy-start | bytes 6291460
  1.6 1.0 copy-start.1
  2.6 0.7 copy-start.2
  3.3 0.7 copy-start.3

commit v2 on v1

v2 whole, which is shorter than its diff:
```python
import functools
import math

import jax
import jax.numpy as jnp
from jax import lax
from jax.experimental import pallas as pl
from jax.experimental.pallas import tpu as pltpu
from jax.sharding import PartitionSpec as P

MESH = pl.DeviceIdType.MESH
GROUP = 8
ALL = (1, -1, 2, -2, 3, -3, 4)


def kernel(n, coeffs, tbox_hbm, sbox_hbm, interp_hbm, out, tbox, sbox, interp, got, tab,
           tabs, waves, phase, wcat, send, recv, tsend, trecv, known, local):
    stride = n // GROUP
    me = lax.axis_index("pairs")
    e_me = me // stride
    rest = me % stride

    def block(d):
        return (e_me + d + GROUP) % GROUP

    def remote(src, dst, ssem, rsem, d):
        return pltpu.make_async_remote_copy(
            src_ref=src, dst_ref=dst, send_sem=ssem, recv_sem=rsem,
            device_id=(block(d) * stride + rest,), device_id_type=MESH,
        )

    def slot_copy(d, g):
        return remote(coeffs.at[block(d) * GROUP + g], got.at[d % GROUP, g],
                      send.at[d % GROUP, g], recv.at[d % GROUP, g], d)

    def table_copy(d):
        return remote(tab, tabs.at[d % GROUP], tsend.at[d % GROUP], trecv.at[d % GROUP], d)

    def tell(sem, d):
        pl.semaphore_signal(known.at[sem], inc=1, device_id=(block(d) * stride + rest,),
                            device_id_type=MESH)

    def for_slots(first, last, moves):
        def step(g, carry):
            for d in moves:
                slot_copy(d, g).start()
            return carry
        lax.fori_loop(first, last, step, 0)

    barrier = pltpu.get_barrier_semaphore()
    for d in (1, -1):
        pl.semaphore_signal(barrier, inc=1, device_id=(block(d) * stride + rest,),
                            device_id_type=MESH)
    boxes = [
        pltpu.make_async_copy(tbox_hbm, tbox, local.at[0]),
        pltpu.make_async_copy(sbox_hbm, sbox, local.at[1]),
    ]
    own_copy = pltpu.make_async_copy(
        coeffs.at[pl.ds(e_me * GROUP, GROUP)], got.at[0], local.at[2]
    )
    weights_copy = pltpu.make_async_copy(interp_hbm, interp, local.at[3])
    for copy in boxes:
        copy.start()
    own_copy.start()
    weights_copy.start()
    for copy in boxes:
        copy.wait()
    turn = (tbox[...] - sbox[...]) & 4095
    tab[0:1, :] = jnp.concatenate([turn[0:1], turn[1:2]], axis=1)
    tab[1:2, :] = jnp.concatenate([turn[2:3], turn[2:3]], axis=1)
    tabs[0] = tab[...]

    pl.semaphore_wait(barrier, 2)
    tell(0, 1)
    tell(1, -1)
    for d in (1, -1):
        table_copy(d).start()
    for_slots(4, 8, (1, -1))
    pl.semaphore_wait(known.at[0], 1)
    pl.semaphore_wait(known.at[1], 1)
    tell(2, 1)
    tell(3, -1)
    for d in (2, -2):
        table_copy(d).start()
    for_slots(6, 8, (2, -2))
    pl.semaphore_wait(known.at[2], 1)
    pl.semaphore_wait(known.at[3], 1)
    tell(4, 1)
    for d in (3, -3):
        table_copy(d).start()
    pl.semaphore_wait(known.at[4], 1)
    table_copy(4).start()
    for_slots(0, 4, (4, 3, -3, 2, -2, 1, -1))
    for_slots(4, 6, (4, 3, -3, 2, -2))
    for_slots(6, 8, (4, 3, -3))

    weights_copy.wait()
    for l in range(3):
        for t in range(2):
            for c in range(2):
                wcat[l, c * 128:(c + 1) * 128, t * 128:(t + 1) * 128] = interp[l, t, c]

    for d in ALL:
        table_copy(d).wait_recv()
    angle = tabs[...].astype(jnp.float32) * (2.0 * math.pi / 4096.0)
    waves[0] = jnp.cos(angle)
    waves[1] = jnp.sin(angle)
    to_scalar = pltpu.make_async_copy(waves, phase, local.at[4])
    to_scalar.start()
    to_scalar.wait()
    own_copy.wait()

    sign = jnp.where(lax.broadcasted_iota(jnp.int32, (1, 128), 1) < 64, -1.0, 1.0)
    f0, f1, f2 = e_me // 4, e_me // 2 % 2, e_me % 2

    def turned(x, e, l, slot):
        at = (e_me - e + GROUP) % GROUP
        c = phase[0, at, l // 2, l % 2 * 64 + slot]
        s = phase[1, at, l // 2, l % 2 * 64 + slot]
        return (c * x + (s * sign) * pltpu.roll(x, 64, 1)).astype(jnp.bfloat16)

    def level(l, pieces):
        rows = jnp.concatenate([jnp.concatenate(p, axis=1) for p in pieces], axis=0)
        return jnp.dot(rows, wcat[l], preferred_element_type=jnp.float32)

    def work(g, carry):
        for d in ALL:
            slot_copy(d, g).wait_recv()
        y = level(0, [
            [turned(got[(e_me - e + GROUP) % GROUP, g].astype(jnp.float32), e, 0,
                    e_me * 8 + g)
             for e in (e1 * 2 + e2, 4 + e1 * 2 + e2)]
            for e1 in range(2) for e2 in range(2)
        ])
        y = level(1, [
            [turned(y[(e1 * 2 + e2) * 128:(e1 * 2 + e2 + 1) * 128, t0 * 128:(t0 + 1) * 128],
                    f0 * 4 + e1 * 2 + e2, 1, f1 * 32 + f2 * 16 + g * 2 + t0)
             for e1 in range(2)]
            for e2 in range(2) for t0 in range(2)
        ])
        y = level(2, [
            [turned(y[(e2 * 2 + t0) * 128:(e2 * 2 + t0 + 1) * 128, t1 * 128:(t1 + 1) * 128],
                    f0 * 4 + f1 * 2 + e2, 2, f2 * 32 + g * 4 + t0 * 2 + t1)
             for e2 in range(2)]
            for t0 in range(2) for t1 in range(2)
        ])
        for t01 in range(4):
            for t2 in range(2):
                out[g * 8 + t01 * 2 + t2] = y[
                    t01 * 128:(t01 + 1) * 128, t2 * 128:(t2 + 1) * 128
                ].astype(jnp.bfloat16)
        return carry

    lax.fori_loop(0, GROUP, work, 0)

    for d in ALL:
        table_copy(d).wait_send()

    def finish(g, carry):
        for d in ALL:
            slot_copy(d, g).wait_send()
        return carry

    lax.fori_loop(0, GROUP, finish, 0)


def solution(mesh):
    n = mesh.shape["pairs"]

    def body(coeffs, target_box, source_box, interp):
        _, rows, columns = coeffs.shape
        dma = pltpu.SemaphoreType.DMA
        return pl.pallas_call(
            functools.partial(kernel, n),
            out_shape=pltpu.VMEM(coeffs.shape, jnp.bfloat16),
            in_specs=[pl.BlockSpec(memory_space=pltpu.HBM)] * 4,
            out_specs=pl.BlockSpec(memory_space=pltpu.VMEM),
            scratch_shapes=[
                pltpu.VMEM(target_box.shape, jnp.int32),
                pltpu.VMEM(source_box.shape, jnp.int32),
                pltpu.VMEM(interp.shape, jnp.bfloat16),
                pltpu.VMEM((GROUP, GROUP, rows, columns), jnp.bfloat16),
                pltpu.VMEM((2, 128), jnp.int32),
                pltpu.VMEM((GROUP, 2, 128), jnp.int32),
                pltpu.VMEM((2, GROUP, 2, 128), jnp.float32),
                pltpu.SMEM((2, GROUP, 2, 128), jnp.float32),
                pltpu.VMEM((3, 256, 256), jnp.bfloat16),
                dma((GROUP, GROUP)),
                dma((GROUP, GROUP)),
                dma((GROUP,)),
                dma((GROUP,)),
                pltpu.SemaphoreType.REGULAR((5,)),
                dma((5,)),
            ],
            compiler_params=pltpu.CompilerParams(
                collective_id=0, has_side_effects=True, vmem_limit_bytes=32 << 20
            ),
            name="butterfly",
        )(*(
            pltpu.with_memory_space_constraint(a, pltpu.HBM)
            for a in (coeffs, target_box, source_box, interp)
        ))

    placed = (P("pairs", None, None), P(None, "pairs"), P(None, "pairs"), P())
    return jax.shard_map(
        body, mesh=mesh, in_specs=placed, out_specs=P("pairs", None, None), check_vma=False
    )
```

time: 116 us -> 107 us (0.922)
  Pallas kernels: 110 us -> 105 us
  local copies, waits for them, and re-layouts: 5.27 us -> 1.32 us
    pallas_call x1, Pallas kernels: 110 us -> 105 us  [body(): pl.pallas_call(functools.partial(kernel, n), out_shape=pltpu.VMEM(coeffs....]
    unnamed x9 -> x1, local copies, waits for them, and re-layouts: 5.27 us -> 1.32 us
where the time goes in v2:
time: 107 us; the launch traced here: 106 us
  Pallas kernels  105 us (98%)
  local copies, waits for them, and re-layouts  1.32 us (1%)
    pallas_call x1, Pallas kernels, body(): pl.pallas_call(functools.partial(kernel, n), out_shape=pltpu.VMEM(coeffs....  105 us

profile of v2, /device:TPU:1, one launch (start us, length us, event | category | flops | bytes accessed | tf_op | source)
XLA Modules:
  0.0 106.4 jit_solution(2681937988108849725)
XLA Ops:
  0.0 105.1 %butterfly.1 = bf16[64,128,128]{2,1,0:T(8,128)(2,1)S(1)} custom-call(bf16[64,128,128]{2,1,0:T(8,128)(2,1)} %coeffs.1, s32[3,64]{1,0:T(4,128)} %tbox_hbm.1, s32[3,64]{1,0:T(4,128)} %sbox_hbm.1, bf16[3,2,2,128,128]{4,3,2,1,0:T(8,128)(2,1)} %interp_hbm.1), custom_call_target="tpu_custom_call" | custom-call | tf_op jit(solution)/shard_map/butterfly/pallas_call | solution.py:173
  105.1 1.3 %copy.6 = bf16[64,128,128]{2,1,0:T(8,128)(2,1)} copy(bf16[64,128,128]{2,1,0:T(8,128)(2,1)S(1)} %butterfly.1) | data formatting | bytes 4194304

commit v3 on v2

--- a/solution.py
+++ b/solution.py
@@ -10,6 +10,7 @@
 
 MESH = pl.DeviceIdType.MESH
 GROUP = 8
+LATER = ((2, 6, 8, 10, 24, 22, 20, 20), (2, 5, 8, 10, 24, 28, 28, 20))
 ALL = (1, -1, 2, -2, 3, -3, 4)
 
 
@@ -46,6 +47,27 @@
                 slot_copy(d, g).start()
             return carry
         lax.fori_loop(first, last, step, 0)
+
+    def wait_of(d):
+        odd = rest // (stride // 2)
+        wait = 0
+        for parity, row in enumerate(LATER):
+            for f, steps in enumerate(row):
+                hit = jnp.logical_and(odd == parity, block(d) == f)
+                wait = jnp.where(hit, steps, wait)
+        return wait
+
+    def in_order(moves):
+        lags = [wait_of(d) for d, _ in moves]
+
+        def step(k, carry):
+            for (d, count), lag in zip(moves, lags):
+                g = k - lag
+                @pl.when(jnp.logical_and(g >= 0, g < count))
+                def _(d=d, g=g):
+                    slot_copy(d, g).start()
+            return carry
+        lax.fori_loop(0, GROUP + max(map(max, LATER)), step, 0)
 
     barrier = pltpu.get_barrier_semaphore()
     for d in (1, -1):
@@ -90,9 +112,7 @@
         table_copy(d).start()
     pl.semaphore_wait(known.at[4], 1)
     table_copy(4).start()
-    for_slots(0, 4, (4, 3, -3, 2, -2, 1, -1))
-    for_slots(4, 6, (4, 3, -3, 2, -2))
-    for_slots(6, 8, (4, 3, -3))
+    in_order(((4, 8), (3, 8), (-3, 8), (2, 6), (-2, 6), (1, 4), (-1, 4)))
 
     weights_copy.wait()
     for l in range(3):

time: 107 us -> 105 us (0.981)
  the two profiles are of different devices: /device:TPU:1 before, /device:TPU:112 now
where the time goes in v3:
time: 105 us; the launch traced here: 104 us
  Pallas kernels  103 us (98%)
  local copies, waits for them, and re-layouts  1.32 us (1%)
    pallas_call x1, Pallas kernels, body(): pl.pallas_call(functools.partial(kernel, n), out_shape=pltpu.VMEM(coeffs....  103 us

profile of v3, /device:TPU:112, one launch (start us, length us, event | category | flops | bytes accessed | tf_op | source)
XLA Modules:
  0.0 104.4 jit_solution(16573572263615780847)
XLA Ops:
  0.0 103.1 %butterfly.1 = bf16[64,128,128]{2,1,0:T(8,128)(2,1)S(1)} custom-call(bf16[64,128,128]{2,1,0:T(8,128)(2,1)} %coeffs.1, s32[3,64]{1,0:T(4,128)} %tbox_hbm.1, s32[3,64]{1,0:T(4,128)} %sbox_hbm.1, bf16[3,2,2,128,128]{4,3,2,1,0:T(8,128)(2,1)} %interp_hbm.1), custom_call_target="tpu_custom_call" | custom-call | tf_op jit(solution)/shard_map/butterfly/pallas_call | solution.py:193
  103.1 1.3 %copy.6 = bf16[64,128,128]{2,1,0:T(8,128)(2,1)} copy(bf16[64,128,128]{2,1,0:T(8,128)(2,1)S(1)} %butterfly.1) | data formatting | bytes 4194304

commit v4 on v3

--- a/solution.py
+++ b/solution.py
@@ -112,7 +112,7 @@
         table_copy(d).start()
     pl.semaphore_wait(known.at[4], 1)
     table_copy(4).start()
-    in_order(((4, 8), (3, 8), (-3, 8), (2, 6), (-2, 6), (1, 4), (-1, 4)))
+    in_order(((-3, 8), (3, 8), (-2, 6), (2, 6), (4, 8), (-1, 4), (1, 4)))
 
     weights_copy.wait()
     for l in range(3):

time: 105 us -> 105 us (level)
  the two profiles are of different devices: /device:TPU:112 before, /device:TPU:192 now
where the time goes in v4:
time: 105 us
  Pallas kernels  103 us (98%)
  local copies, waits for them, and re-layouts  1.32 us (1%)
    pallas_call x1, Pallas kernels, body(): pl.pallas_call(functools.partial(kernel, n), out_shape=pltpu.VMEM(coeffs....  103 us

profile of v4, /device:TPU:192, one launch (start us, length us, event | category | flops | bytes accessed | tf_op | source)
XLA Modules:
  0.0 104.6 jit_solution(9269487892740640469)
XLA Ops:
  0.0 103.3 %butterfly.1 = bf16[64,128,128]{2,1,0:T(8,128)(2,1)S(1)} custom-call(bf16[64,128,128]{2,1,0:T(8,128)(2,1)} %coeffs.1, s32[3,64]{1,0:T(4,128)} %tbox_hbm.1, s32[3,64]{1,0:T(4,128)} %sbox_hbm.1, bf16[3,2,2,128,128]{4,3,2,1,0:T(8,128)(2,1)} %interp_hbm.1), custom_call_target="tpu_custom_call" | custom-call | tf_op jit(solution)/shard_map/butterfly/pallas_call | solution.py:193
  103.3 1.3 %copy.6 = bf16[64,128,128]{2,1,0:T(8,128)(2,1)} copy(bf16[64,128,128]{2,1,0:T(8,128)(2,1)S(1)} %butterfly.1) | data formatting | bytes 4194304
